TPU v7x, 32 devices: a whole 2x2x4 slice. The times are simulated.
32 devices in a mesh: groups: 2 (over x), ctx: 16 (over z, y, core).
Axes of the slice: x: 2, y: 2, z: 4, core: 2. Of those that a mesh axis runs over, the one named last changes fastest.
Arguments:
- projected: bfloat16 [4096, 6144], P(('groups', 'ctx')), parts along dimension 0, may hold values from -6 to 6
- short_filter: float32 [3, 6144], replicated, may hold values from -3.5 to 3.5
- modal_pole: float32 [2048, 16], replicated, may hold values from 0.96 to 1, as said below
- residue: float32 [2048, 16], replicated, may hold values from -1.5 to 1.5
- skip_weight: float32 [2048], replicated, may hold values from -3 to 3
- out_weight: bfloat16 [2048, 4096], P('ctx'), may hold values from -0.125 to 0.125
Outputs:
- block_output: bfloat16 [4096, 4096], P(('groups', 'ctx')), parts along dimension 0
There are 2 independent parts, one for each index of `groups`. A program takes and returns all parts, laid end to end along the dimension named above; an argument that names none is the same for every part. Nothing has to cross between parts.
Inputs may be any that keep to these rules, and one draw needn't show every extreme that they name: `modal_pole`: every pole lies strictly between 0 and 1.
All inputs are finite; a program needn't handle non-finite values.
Results may differ from a plain program's by a relative error of at most 0.005.
Values may be sent and summed in bfloat16 or wider, within the bound.
A program may use at most 128 MiB of HBM per device.

v0:
```python
import jax
import jax.numpy as jnp
from jax import lax
from jax.sharding import PartitionSpec as P

BLOCK = 16


def passed_along(x, axis, by):
    length = lax.axis_size(axis)
    pairs = [(i, i + by) for i in range(length) if 0 <= i + by < length]
    return lax.ppermute(x, axis, pairs)


def local(projected, short_filter, modal_pole, residue, skip_weight, out_weight):
    tok_rows = projected.shape[0]
    chan_count = modal_pole.shape[0]
    rim_rows = passed_along(projected[tok_rows - 2 :], "ctx", 1)
    extended = jnp.concatenate([rim_rows, projected], 0).astype(jnp.float32)
    smoothed = (
        short_filter[0] * extended[2:]
        + short_filter[1] * extended[1:-1]
        + short_filter[2] * extended[:-2]
    )
    query_part = smoothed[:, :chan_count]
    drive = smoothed[:, chan_count : 2 * chan_count] * smoothed[:, 2 * chan_count :]
    pole_rows = modal_pole.T
    residue_rows = residue.T
    input_gain = jnp.sqrt((1.0 - pole_rows) * (1.0 + pole_rows))
    log_pole = jnp.log(pole_rows)
    block_count = tok_rows // BLOCK
    positions = jnp.arange(BLOCK)
    powers = jnp.exp(positions.astype(jnp.float32)[:, None, None] * log_pole[None])
    powers_next = powers * pole_rows[None]
    powers_back = powers[::-1]
    block_decay = jnp.exp(jnp.float32(BLOCK) * log_pole)
    kernel = jnp.sum(powers * (residue_rows * input_gain)[None], 1)
    lag_steps = positions[:, None] - positions[None, :]
    toeplitz = jnp.where(lag_steps[:, :, None] >= 0, kernel[jnp.maximum(lag_steps, 0)], 0.0)
    drive_blocks = drive.reshape(block_count, BLOCK, chan_count)

    def local_step(modal_state, drive_block):
        partial_value = jnp.sum(toeplitz * drive_block[None], 1)
        partial_value = partial_value + jnp.sum(powers_next * (modal_state * residue_rows)[None], 1)
        gathered_in = jnp.sum(powers_back * drive_block[:, None, :], 0)
        modal_state = block_decay * modal_state + input_gain * gathered_in
        return (modal_state, partial_value)

    empty_state = jnp.zeros(pole_rows.shape, jnp.float32)
    state_end, partials = lax.scan(local_step, empty_state, drive_blocks)
    my_index = lax.axis_index("ctx")
    shard_rows = lax.all_gather(state_end[None], "ctx", axis=0, tiled=True)
    shard_count = shard_rows.shape[0]
    source = jnp.arange(shard_count)
    distance = (my_index - 1 - source).astype(jnp.float32)
    weight = jnp.where(
        distance[:, None, None] >= 0.0,
        jnp.exp(jnp.maximum(distance, 0.0)[:, None, None] * jnp.float32(tok_rows) * log_pole[None]),
        0.0,
    )
    state_start = jnp.sum(weight * shard_rows, 0)
    block_starts = (jnp.arange(block_count) * BLOCK).astype(jnp.float32)
    offsets = jnp.exp(block_starts[:, None, None] * log_pole[None])
    coefficient = offsets * (residue_rows * state_start)[None]
    carried = jnp.sum(powers_next[None] * coefficient[:, None], 2)
    filtered = (partials + carried).reshape(tok_rows, chan_count) + skip_weight * drive
    gated_rows = (query_part * filtered).astype(jnp.bfloat16)
    whole_weight = lax.all_gather(out_weight, "ctx", axis=0, tiled=True)
    block_output = jnp.dot(gated_rows, whole_weight, preferred_element_type=jnp.float32)
    return block_output.astype(jnp.bfloat16)


def solution(mesh):
    placed = (P(("groups", "ctx"), None), P(), P(), P(), P(), P("ctx", None))
    return jax.shard_map(
        local, mesh=mesh, in_specs=placed, out_specs=P(("groups", "ctx"), None), check_vma=False
    )
```

profile of v0, /device:TPU:1, one launch (start us, length us, event | category | flops | bytes accessed | tf_op | source)
XLA Modules:
  0.0 251.6 jit_solution(10597921108877451209)
XLA Ops:
  6.5 0.9 slice.31
  7.5 4.5 %collective-permute-start = (bf16[2,6144]{1,0:T(2,128)(2,1)S(1)}, bf16[2,6144]{1,0:T(2,128)(2,1)S(1)}, u32[]{:S(2)}, u32[]{:S(2)}) collective-permute-start(bf16[2,6144]{1,0:T(2,128)(2,1)S(1)} %slice.31), channel_id=1, source_target_pairs={{0,1},{1,2},{2,3},{3,4},{4,5},{5,6},{6,7},{7,8},{8,9},{9,10},{10,1... | collective-permute-start | bytes 73736 | tf_op jit(solution)/shard_map/ppermute | solution.py:12
  12.1 1.1 fusion.7
  13.3 1.0 bitcast_multiply_fusion.1
  14.3 3.6 %fusion.5 = (f32[16,16,2048]{2,1,0:T(8,128)}, f32[16,2048]{1,0:T(8,128)S(1)}, f32[16,16,2048]{2,1,0:T(8,128)}) fusion(f32[16,2048]{1,0:T(8,128)} %bitcast.37, f32[16,2048]{1,0:T(8,128)S(1)} %get-tuple-element.232, f32[16]{0:T(128)S(1)} %iota_convert_fusion, f32[16,2048]{1,0:T(8,128)S(1)} %get-tuple-element.135), kind=kLoop, calls=%fused_computation.21 | loop fusion | flops 2064384 | bytes 4718656 | tf_op jit(solution)/shard_map/mul | solution.py:34
  17.9 1.5 gather_fusion
  19.4 1.5 broadcast_select_fusion
  20.9 1.7 rev.3
  22.7 1.9 maximum_convert_fusion
  24.6 0.9 fusion.3
  25.5 1.6 copy-done
  27.1 1.1 slice_multiply_fusion.3
  28.3 37.1 %while.13 = (s32[]{:T(128)}, f32[16,2048]{1,0:T(8,128)S(1)}, f32[8,16,2048]{2,1,0:T(8,128)}, f32[16,2048]{1,0:T(8,128)S(1)}, f32[8,16,2048]{2,1,0:T(8,128)}, /*i...) while((s32[]{:T(128)}, f32[16,2048]{1,0:T(8,128)S(1)}, ...), condition=%wide.region_5.6_spmd.clone, body=%wide.region_1.5_spmd.clone.sunk | while | flops 4292611 | bytes 6685395 | solution.py:50
  28.3 0.9 dynamic-slice_bitcast_fusion.2
  29.2 2.3 multiply_reduce_fusion.6
  31.4 0.1 select_multiply_fusion.2
  31.5 0.7 fusion.11
  32.2 0.7 bitcast_dynamic-update-slice_fusion.2
  32.9 0.9 dynamic-slice_bitcast_fusion.2
  33.8 2.3 multiply_reduce_fusion.6
  36.1 0.1 select_multiply_fusion.2
  36.2 0.7 fusion.11
  36.9 0.7 bitcast_dynamic-update-slice_fusion.2
  37.5 0.9 dynamic-slice_bitcast_fusion.2
  38.5 2.3 multiply_reduce_fusion.6
  40.7 0.1 select_multiply_fusion.2
  40.8 0.7 fusion.11
  41.5 0.7 bitcast_dynamic-update-slice_fusion.2
  42.2 0.9 dynamic-slice_bitcast_fusion.2
  43.1 2.3 multiply_reduce_fusion.6
  45.4 0.1 select_multiply_fusion.2
  45.5 0.7 fusion.11
  46.1 0.7 bitcast_dynamic-update-slice_fusion.2
  46.8 0.9 dynamic-slice_bitcast_fusion.2
  47.7 2.3 multiply_reduce_fusion.6
  50.0 0.1 select_multiply_fusion.2
  50.1 0.7 fusion.11
  50.8 0.7 bitcast_dynamic-update-slice_fusion.2
  51.5 0.9 dynamic-slice_bitcast_fusion.2
  52.4 2.3 multiply_reduce_fusion.6
  54.7 0.1 select_multiply_fusion.2
  54.7 0.7 fusion.11
  55.4 0.7 bitcast_dynamic-update-slice_fusion.2
  56.1 0.9 dynamic-slice_bitcast_fusion.2
  57.0 2.3 multiply_reduce_fusion.6
  59.3 0.1 select_multiply_fusion.2
  59.4 0.7 fusion.11
  60.1 0.7 bitcast_dynamic-update-slice_fusion.2
  60.7 0.9 dynamic-slice_bitcast_fusion.2
  61.7 2.3 multiply_reduce_fusion.6
  64.0 0.7 fusion.11
  64.7 0.7 bitcast_dynamic-update-slice_fusion.2
  65.4 0.6 copy-done.4
  66.1 0.2 all-gather.4.cloned.1.call-start
  66.3 0.5 all-gather.4.cloned.1.call-update
  66.9 40.9 %all-gather.6.cloned.1.call-done = f32[256,2048]{1,0:T(8,128)} async-done(((f32[16,2048]{1,0:T(8,128)}), f32[256,2048]{1,0:T(8,128)}) %all-gather.6.cloned.1.call-update) | async-done | bytes 2097168 | tf_op jit(solution)/shard_map/all_gather | solution.py:52
  107.8 2.1 multiply_reduce_fusion.3
  109.9 0.2 exponential_multiply_fusion
  110.2 4.2 %multiply_reduce_fusion.2 = f32[8,16,2048]{2,1,0:T(8,128)S(1)} fusion(f32[8,16,2048]{2,1,0:T(8,128)S(1)} %exponential_multiply_fusion, f32[16,16,2048]{2,1,0:T(8,128)S(1)} %copy-done.2), kind=kLoop, calls=%fused_computation.10 | loop fusion | flops 8126464 | bytes 4194304 | tf_op jit(solution)/shard_map/reduce_sum | solution.py:65
  114.4 0.1 add.40
  114.5 1.9 copy-done.1
  116.4 0.3 fusion.6
  116.7 119.0 %all-gather.4.cloned.1.call-done = bf16[2048,4096]{1,0:T(8,128)(2,1)} async-done(((bf16[128,4096]{1,0:T(8,128)(2,1)}), bf16[2048,4096]{1,0:T(8,128)(2,1)}) %all-gather.4.cloned.1.call-update) | async-done | bytes 16777232 | tf_op jit(solution)/shard_map/all_gather | solution.py:68
  235.7 9.1 %convolution_convert_fusion = bf16[128,4096]{1,0:T(8,128)(2,1)} fusion(bf16[128,2048]{1,0:T(8,128)(2,1)S(1)} %fusion.6, bf16[2048,4096]{1,0:T(8,128)(2,1)} %all-gather.4.cloned.1.call-done), kind=kOutput, calls=%fused_computation.11 | convolution fusion | flops 2148007936 | bytes 18350080 | tf_op jit(solution)/shard_map/dot_general | solution.py:69
  (28 shorter events, 0.3 us)
Async XLA Ops:
  6.5 101.3 %all-gather.6.cloned.1.call-start = ((), (), s32[]{:S(2)}) async-start(), calls=%async_computation.1 | async-start | bytes 2228224 | tf_op jit(solution)/shard_map/all_gather | solution.py:52
  7.5 15.2 %collective-permute-start = (bf16[2,6144]{1,0:T(2,128)(2,1)S(1)}, bf16[2,6144]{1,0:T(2,128)(2,1)S(1)}, u32[]{:S(2)}, u32[]{:S(2)}) collective-permute-start(bf16[2,6144]{1,0:T(2,128)(2,1)S(1)} %slice.31), channel_id=1, source_target_pairs={{0,1},{1,2},{2,3},{3,4},{4,5},{5,6},{6,7},{7,8},{8,9},{9,10},{10,1... | collective-permute-start | bytes 73736 | tf_op jit(solution)/shard_map/ppermute | solution.py:12
  25.5 1.6 copy-start
  27.1 1.1 copy-start.3
  27.1 1.1 copy-start.6
  65.4 0.6 copy-start.4
  66.1 169.6 %all-gather.4.cloned.1.call-start = ((), (), s32[]{:S(2)}) async-start(), calls=%async_computation | async-start | bytes 17825792 | tf_op jit(solution)/shard_map/all_gather | solution.py:68
  66.8 43.3 %copy-start.2 = (f32[16,16,2048]{2,1,0:T(8,128)S(1)}, f32[16,16,2048]{2,1,0:T(8,128)}, u32[]{:S(2)}) copy-start(f32[16,16,2048]{2,1,0:T(8,128)} %get-tuple-element.132) | copy-start | bytes 6291460
  110.2 4.2 %copy-start.5 = (f32[8,16,2048]{2,1,0:T(8,128)S(1)}, f32[8,16,2048]{2,1,0:T(8,128)}, u32[]{:S(2)}) copy-start(f32[8,16,2048]{2,1,0:T(8,128)} %get-tuple-element.58) | copy-start | bytes 3145732
  110.2 4.3 %copy-start.7 = (f32[2048]{0:T(1024)S(1)}, f32[2048]{0:T(1024)}, u32[]{:S(2)}) copy-start(f32[2048]{0:T(1024)} %param.12) | copy-start | bytes 24580
  114.3 2.1 copy-start.1
Sparse Core Ops, SparseCore 0:
  66.2 41.5 all-gather.5
  110.0 125.6 all-gather.3
where the time goes:
time: 253 us; the launch traced here: 252 us
  waiting for transfers between devices  160 us (63%)
  other arithmetic  46.7 us (18%)
  local copies, waits for them, and re-layouts  16.8 us (7%)
  between operations  13.6 us (5%)
  matrix products  9.08 us (4%)
  starting transfers between devices  4.76 us (2%)
    all_gather x1, waiting for transfers between devices, local(): whole_weight = lax.all_gather(out_weight, 'ctx', axis=0, tiled=True)  119 us
    all_gather x1, waiting for transfers between devices, local(): shard_rows = lax.all_gather(state_end[None], 'ctx', axis=0, tiled=True)  40.9 us
    reduce_sum x8, other arithmetic, local_step(): partial_value = jnp.sum(toeplitz * drive_block[None], 1)  18.1 us
    dot_general x1, matrix products, local(): jnp.dot(gated_rows, whole_weight, preferred_element_type=jnp.float32)  9.08 us
    mul x8, local copies, waits for them, and re-layouts, local_step(): gathered_in = jnp.sum(powers_back * drive_block[:, None, :], 0)  7.31 us
    reduce_sum x8, other arithmetic, local_step(): jnp.sum(powers_next * (modal_state * residue_rows)[None], 1)  5.44 us
    dynamic_update_slice x8, other arithmetic, local(): state_end, partials = lax.scan(local_step, empty_state, drive_blocks)  5.41 us
  transfers between devices with their start and end apart: 3, of which 2 were waited for; matrix products, arithmetic and copies ran while one was open for 7% of the time, Pallas kernels for 0%

commit v1 on v0

v1 whole, which is shorter than its diff:
```python
import functools

import jax
import jax.numpy as jnp
from jax import lax
from jax.experimental import pallas as pl
from jax.experimental.pallas import tpu as pltpu
from jax.sharding import PartitionSpec as P

MESH = pl.DeviceIdType.MESH
LANES = 128
PHASES = 4
SKEW = 3


def kernel(
    ctx_count, proj, taps, pole, res, skip, w_in, out,
    halo, pole_t, coef_t, decay, drive, filt, query, sent, came, gated, w_all, prod,
    halo_sem, mate_sem, own_sem, ring_send, ring_recv, state_sem, gate_sem, fwd_sem, prod_sem, keep_sem,
):
    group = lax.axis_index("groups")
    ctx = lax.axis_index("ctx")
    core = ctx % 2
    place = ctx // 2
    places = ctx_count // 2
    half = places // 2
    across = group + 1 - 2 * (group % 2)
    other = ctx + 1 - 2 * core
    quarter = (group % 2) * 2 + core
    rank = place // 2 + (place % 2) * (places - 1 - 2 * (place // 2))
    sign = 1 - 2 * core

    tokens = proj.shape[0]
    chans = skip.shape[0] * LANES
    tiles = skip.shape[0]
    poles = pole.shape[0]
    w_rows = w_in.shape[0]
    width = w_in.shape[1] // 4
    cols = width // PHASES
    hops = [1]
    while hops[-1] * 2 < ctx_count:
        hops.append(hops[-1] * 2)

    def place_at(r):
        r = (r + 2 * places) % places
        h = r // half
        return 2 * (r + h * (places - 1 - 2 * r)) + h

    ahead = 2 * place_at(rank + sign) + core
    behind = 2 * place_at(rank - sign) + core

    barrier = pltpu.get_barrier_semaphore()
    greeted = [(group, other), (across, ctx), (across, other), (group, ahead), (group, behind)]
    for hop in hops:
        greeted.append((group, (ctx + hop) % ctx_count))
        greeted.append((group, (ctx + ctx_count - hop) % ctx_count))
    for device in greeted:
        pl.semaphore_signal(barrier, inc=1, device_id=device, device_id_type=MESH)
    pl.semaphore_wait(barrier, len(greeted))

    def remote(src, dst, send, recv, device):
        return pltpu.make_async_remote_copy(
            src_ref=src, dst_ref=dst, send_sem=send, recv_sem=recv,
            device_id=device, device_id_type=MESH,
        )

    pending = []

    def begin(copy):
        copy.start()
        pending.append(copy)
        return copy

    edge = min(16, tokens)
    halo_copy = remote(
        proj.at[pl.ds(tokens - edge, edge)], halo, halo_sem.at[0], halo_sem.at[1],
        (group, (ctx + 1) % ctx_count),
    )

    @pl.when(ctx + 1 < ctx_count)
    def _():
        halo_copy.start()

    my_rows = pl.ds(pl.multiple_of(ctx * w_rows, w_rows), w_rows)
    other_rows = pl.ds(pl.multiple_of(other * w_rows, w_rows), w_rows)
    their_quarter = (group % 2) * 2 + 1 - core

    def part(q, s):
        return pl.ds(pl.multiple_of(q * width + s * cols, cols), cols)

    mate_copies = []
    own_copies = []
    for s in range(PHASES):
        mate_copies.append(begin(remote(
            w_in.at[:, part(their_quarter, s)], w_all.at[s, my_rows],
            mate_sem.at[0, s], mate_sem.at[1, s], (group, other),
        )))
        own = pltpu.make_async_copy(w_in.at[:, part(quarter, s)], w_all.at[s, my_rows], own_sem.at[s])
        own.start()
        own_copies.append(own)

    def ring_copy(d, s, t):
        if d == 0:
            origin = 2 * place_at(rank - sign * t) + core
            device = (group, ahead)
        else:
            origin = 2 * place_at(rank + sign * t) + 1 - core
            device = (group, behind)
        rows = pl.ds(pl.multiple_of(origin * w_rows, w_rows), w_rows)
        dst = w_all.at[s, rows]
        src = w_in.at[:, part(quarter, s)] if d == 0 and t == 0 else dst
        return remote(src, dst, ring_send.at[d, s, t], ring_recv.at[d, s, t], device)

    ring = {}

    def event(s, t):
        for d in range(2):
            if t > 0:
                ring[d, s, t - 1].wait_recv()
            elif d == 1:
                mate_copies[s].wait_recv()
            if t < places - 1:
                ring[d, s, t] = begin(ring_copy(d, s, t))

    events = sorted(
        [(t + SKEW * s, s, t) for s in range(PHASES) for t in range(places)]
    )
    done = [0]

    def run_events(n):
        for _ in range(n):
            if done[0] < len(events):
                _, s, t = events[done[0]]
                event(s, t)
                done[0] += 1

    def phase_over(s):
        return events.index((places - 1 + SKEW * s, s, places - 1)) + 1

    run_events(3)

    def spread(c, carry):
        lanes = pl.ds(pl.multiple_of(c * LANES, LANES), LANES)
        p = pole[:, lanes]
        gain = jnp.sqrt((1.0 - p) * (1.0 + p))
        rows = pl.ds(c, poles, stride=tiles)
        pole_t[rows, :] = p
        coef_t[rows, :] = res[:, lanes] * gain
        left = tokens
        power = p
        total = None
        while left:
            if left & 1:
                total = power if total is None else total * power
            left >>= 1
            if left:
                power = power * power
        decay[rows, :] = total
        return carry

    lax.fori_loop(0, tiles, spread, 0)

    @pl.when(ctx > 0)
    def _():
        halo_copy.wait_recv()

    @pl.when(ctx == 0)
    def _():
        halo[...] = jnp.zeros(halo.shape, halo.dtype)

    row = lax.broadcasted_iota(jnp.int32, (tokens, LANES), 0)

    def smooth(col):
        lanes = pl.ds(pl.multiple_of(col, LANES), LANES)
        x = proj[:, lanes].astype(jnp.float32)
        rim = halo[:, lanes].astype(jnp.float32)
        near = rim[edge - 1 : edge]
        far = rim[edge - 2 : edge - 1]
        back1 = jnp.where(row == 0, near, pltpu.roll(x, 1, 0))
        back2 = jnp.where(row == 0, far, jnp.where(row == 1, near, pltpu.roll(x, 2, 0)))
        return taps[0:1, lanes] * x + taps[1:2, lanes] * back1 + taps[2:3, lanes] * back2

    def make_drive(c, carry):
        drive[pl.ds(c, tokens, stride=tiles), :] = smooth(chans + c * LANES) * smooth(2 * chans + c * LANES)
        return carry

    def make_query(c, carry):
        query[:, pl.ds(pl.multiple_of(c * LANES, LANES), LANES)] = smooth(c * LANES)
        return carry

    pieces = tiles // 8

    def end_state(h):
        p = [pole_t[n * tiles + h * 8 : n * tiles + h * 8 + 8] for n in range(poles)]

        def step(t, state):
            d = drive[pl.ds(pl.multiple_of(t * tiles + h * 8, 8), 8)]
            return tuple(p[n] * state[n] + d for n in range(poles))

        zero = tuple(jnp.zeros((8, LANES), jnp.float32) for _ in range(poles))
        state = lax.fori_loop(0, tokens, step, zero, unroll=4)
        for n in range(poles):
            sent[0, n * tiles + h * 8 : n * tiles + h * 8 + 8] = state[n]

    for h in range(pieces):
        lax.fori_loop(h * 8, h * 8 + 8, make_drive, 0)
        run_events(1)
        end_state(h)
        run_events(1)

    def state_copy(slot, buf, hop):
        return remote(
            sent.at[buf], came.at[slot], state_sem.at[0, slot], state_sem.at[1, slot],
            (group, (ctx + hop) % ctx_count),
        )

    state_copies = []

    def state_start(slot, buf, hop):
        copy = state_copy(slot, buf, hop)
        state_copies.append((copy, hop))

        @pl.when(ctx + hop < ctx_count)
        def _():
            copy.start()

        return copy

    first = state_start(0, 0, 1)
    second = state_start(1, 0, 2)
    run_events(1)
    lax.fori_loop(0, tiles // 2, make_query, 0)
    run_events(1)
    sent[1] = jnp.zeros(sent.shape[1:], jnp.float32)

    @pl.when(ctx >= 1)
    def _():
        first.wait_recv()
        sent[1] = came[0]

    @pl.when(ctx >= 2)
    def _():
        second.wait_recv()
        sent[1] = sent[1] + decay[...] * came[1]

    buf = 1
    for k, hop in enumerate(hops[1:]):
        copy = state_start(2 + k, buf, hop)
        decay[...] = decay[...] * decay[...]
        run_events(1)
        if k == 0:
            lax.fori_loop(tiles // 2, tiles, make_query, 0)
        run_events(1)
        sent[buf + 1] = sent[buf]

        @pl.when(ctx >= hop)
        def _():
            copy.wait_recv()
            sent[buf + 1] = sent[buf] + decay[...] * came[2 + k]

        buf += 1

    def respond(h):
        p = [pole_t[n * tiles + h * 8 : n * tiles + h * 8 + 8] for n in range(poles)]
        q = [coef_t[n * tiles + h * 8 : n * tiles + h * 8 + 8] for n in range(poles)]
        direct = skip[h * 8 : h * 8 + 8]

        def step(t, state):
            at = pl.ds(pl.multiple_of(t * tiles + h * 8, 8), 8)
            d = drive[at]
            state = tuple(p[n] * state[n] + d for n in range(poles))
            terms = [q[n] * state[n] for n in range(poles)] + [direct * d]
            while len(terms) > 1:
                terms = [a + b for a, b in zip(terms[::2], terms[1::2])] + terms[len(terms) & ~1 :]
            filt[at] = terms[0]
            return state

        start = tuple(sent[buf, n * tiles + h * 8 : n * tiles + h * 8 + 8] for n in range(poles))
        lax.fori_loop(0, tokens, step, start, unroll=2)

    def gate(c, carry):
        lanes = pl.ds(pl.multiple_of(c * LANES, LANES), LANES)
        value = query[:, lanes] * filt[pl.ds(c, tokens, stride=tiles), :]
        gated[quarter, :, lanes] = value.astype(jnp.bfloat16)
        return carry

    slot_across = (quarter + 2) % 4
    span = chans // pieces
    direct_copies = []
    for h in range(pieces):
        respond(h)
        lax.fori_loop(h * 8, h * 8 + 8, gate, 0)
        mine = gated.at[quarter, :, h * span : (h + 1) * span]
        direct_copies.append((
            begin(remote(mine, mine, gate_sem.at[0, 0, h], gate_sem.at[1, 0, h], (across, ctx))),
            begin(remote(mine, mine, gate_sem.at[0, 1, h], gate_sem.at[1, 1, h], (group, other))),
        ))
        run_events(2)

    forwards = []
    for h in range(pieces):
        run_events(3)
        direct_copies[h][0].wait_recv()
        theirs = gated.at[slot_across, :, h * span : (h + 1) * span]
        forwards.append(begin(remote(theirs, theirs, fwd_sem.at[0, h], fwd_sem.at[1, h], (group, other))))
    run_events(2)
    for h in range(pieces):
        direct_copies[h][1].wait_recv()
        forwards[h].wait_recv()

    mates = [(group, other), (across, ctx), (across, other)]
    mate_slots = [(group % 2) * 2 + 1 - core, slot_across, (across % 2) * 2 + 1 - core]
    returns = []
    keeps = []
    for s in range(PHASES):
        run_events(phase_over(s) - done[0])
        own_copies[s].wait()

        def block(i, carry):
            left = gated[pl.ds(2 * i, 2)].reshape(2 * tokens, chans)
            value = jnp.dot(left, w_all[s], preferred_element_type=jnp.float32)
            prod[s, pl.ds(2 * i, 2)] = value.astype(jnp.bfloat16).reshape(2, tokens, cols)
            return carry

        lax.fori_loop(0, 2, block, 0)
        where = out.at[:, part(quarter, s)]
        for k in (1, 2, 0):
            returns.append(begin(remote(
                prod.at[s, mate_slots[k]], where, prod_sem.at[0, k, s], prod_sem.at[1, k, s], mates[k],
            )))
        keep = pltpu.make_async_copy(prod.at[s, quarter], where, keep_sem.at[s])
        keep.start()
        keeps.append(keep)

    for copy in returns:
        copy.wait_recv()
    for keep in keeps:
        keep.wait()
    for copy in pending:
        copy.wait_send()

    @pl.when(ctx + 1 < ctx_count)
    def _():
        halo_copy.wait_send()

    for copy, hop in state_copies:

        @pl.when(ctx + hop < ctx_count)
        def _():
            copy.wait_send()


def local(ctx_count, projected, short_filter, modal_pole, residue, skip_weight, out_weight):
    tokens = projected.shape[0]
    chans, poles = modal_pole.shape
    w_rows, width = out_weight.shape
    tiles = chans // LANES
    cols = width // 4 // PHASES
    places = ctx_count // 2
    hop_count = (ctx_count - 1).bit_length()
    dma = pltpu.SemaphoreType.DMA
    whole = pl.BlockSpec(memory_space=pltpu.VMEM)
    anywhere = pl.BlockSpec(memory_space=pl.ANY)
    f32, bf16 = jnp.float32, jnp.bfloat16
    pieces = tiles // 8
    return pl.pallas_call(
        functools.partial(kernel, ctx_count),
        out_shape=jax.ShapeDtypeStruct((tokens, width), bf16),
        in_specs=[whole] * 5 + [anywhere],
        out_specs=anywhere,
        scratch_shapes=[
            pltpu.VMEM((min(16, tokens), 3 * chans), bf16),
            pltpu.VMEM((poles * tiles, LANES), f32),
            pltpu.VMEM((poles * tiles, LANES), f32),
            pltpu.VMEM((poles * tiles, LANES), f32),
            pltpu.VMEM((tokens * tiles, LANES), f32),
            pltpu.VMEM((tokens * tiles, LANES), f32),
            pltpu.VMEM((tokens, chans), f32),
            pltpu.VMEM((hop_count + 1, poles * tiles, LANES), f32),
            pltpu.VMEM((hop_count + 1, poles * tiles, LANES), f32),
            pltpu.VMEM((4, tokens, chans), bf16),
            pltpu.VMEM((PHASES, chans, cols), bf16),
            pltpu.VMEM((PHASES, 4, tokens, cols), bf16),
            dma((2,)),
            dma((2, PHASES)),
            dma((PHASES,)),
            dma((2, PHASES, places - 1)),
            dma((2, PHASES, places - 1)),
            dma((2, hop_count + 1)),
            dma((2, 2, pieces)),
            dma((2, pieces)),
            dma((2, 3, PHASES)),
            dma((PHASES,)),
        ],
        compiler_params=pltpu.CompilerParams(
            collective_id=0, has_side_effects=True, vmem_limit_bytes=40 * 1024 * 1024
        ),
    )(
        projected, short_filter, modal_pole.T, residue.T,
        skip_weight.reshape(tiles, LANES), out_weight,
    )


def solution(mesh):
    placed = (P(("groups", "ctx"), None), P(), P(), P(), P(), P("ctx", None))
    return jax.shard_map(
        functools.partial(local, mesh.shape["ctx"]), mesh=mesh, in_specs=placed,
        out_specs=P(("groups", "ctx"), None), check_vma=False,
    )
```

time: 253 us -> 94.3 us (0.37)
  waiting for transfers between devices: 160 us -> 0 us
  Pallas kernels: 0 us -> 87 us
  other arithmetic: 46.7 us -> 0 us
  between operations: 13.6 us -> 0.02 us
  local copies, waits for them, and re-layouts: 16.8 us -> 7 us
  matrix products: 9.08 us -> 0 us
  starting transfers between devices: 4.76 us -> 0 us
    all_gather x2 -> x0, waiting for transfers between devices: 160 us -> none  [the longest x1 119 us: local(): whole_weight = lax.all_gather(out_weight, 'ctx', axis=0, tiled=True)]
    pallas_call x0 -> x1, Pallas kernels: none -> 87 us  [local(): pl.pallas_call(functools.partial(kernel, ctx_count), out_shape=jax.ShapeD...]
    reduce_sum x18 -> x0, other arithmetic: 29.8 us -> none  [the longest x8 18.1 us: local_step(): partial_value = jnp.sum(toeplitz * drive_block[None], 1)]
    dot_general x1 -> x0, matrix products: 9.08 us -> none  [local(): jnp.dot(gated_rows, whole_weight, preferred_element_type=jnp.float32)]
    mul x8 -> x0, local copies, waits for them, and re-layouts: 7.31 us -> none  [local_step(): gathered_in = jnp.sum(powers_back * drive_block[:, None, :], 0)]
    mul x14 -> x0, other arithmetic: 6.74 us -> none  [the longest x1 3.64 us: local(): powers_next = powers * pole_rows[None]]
    dynamic_update_slice x8 -> x0, other arithmetic: 5.41 us -> none  [local(): state_end, partials = lax.scan(local_step, empty_state, drive_blocks)]
    ppermute x1 -> x0, starting transfers between devices: 4.54 us -> none  [passed_along(): return lax.ppermute(x, axis, pairs)]
  transfers between devices with their start and end apart: 3 -> 0, of which waited for: 2 -> 0; matrix products, arithmetic and copies ran while one was open for 7% -> 0% of each run, Pallas kernels for 0% -> 0%
where the time goes in v1:
time: 94.3 us; the launch traced here: 94 us
  Pallas kernels  87 us (92%)
  local copies, waits for them, and re-layouts  7 us (7%)
    pallas_call x1, Pallas kernels, local(): pl.pallas_call(functools.partial(kernel, ctx_count), out_shape=jax.ShapeD...  87 us
    unnamed x13, local copies, waits for them, and re-layouts  7 us

profile of v1, /device:TPU:1, one launch (start us, length us, event | category | flops | bytes accessed | tf_op | source)
XLA Modules:
  0.0 94.0 jit_solution(5563996038602342482)
XLA Ops:
  0.0 0.0 copy-start
  0.0 1.4 %copy-done = bf16[128,6144]{1,0:T(8,128)(2,1)S(1)} copy-done((bf16[128,6144]{1,0:T(8,128)(2,1)S(1)}, bf16[128,6144]{1,0:T(8,128)(2,1)}, u32[]{:S(2)}) %copy-start) | copy-done | bytes 1572888
  1.4 0.0 copy-start.1
  1.4 1.2 %copy-done.1 = bf16[128,4096]{1,0:T(8,128)(2,1)S(1)} copy-done((bf16[128,4096]{1,0:T(8,128)(2,1)S(1)}, bf16[128,4096]{1,0:T(8,128)(2,1)}, u32[]{:S(2)}) %copy-start.1) | copy-done | bytes 1048600
  2.6 0.0 copy-start.2
  2.6 0.9 copy-done.2
  3.5 0.0 copy-start.3
  3.5 0.9 copy-done.3
  4.4 0.0 copy-start.4
  4.4 0.9 copy-done.4
  5.3 0.0 copy-start.5
  5.3 0.7 copy-done.5
  6.0 87.0 %shard_map.64 = bf16[128,4096]{1,0:T(8,128)(2,1)S(1)} custom-call(bf16[128,6144]{1,0:T(8,128)(2,1)S(1)} %copy-done, f32[3,6144]{1,0:T(4,128)S(1)} %copy-done.4, f32[16,2048]{1,0:T(8,128)S(1)} %bitcast.3, f32[16,2048]{1,0:T(8,128)S(1)} %bitcast.4, f32[16,128]{1,0:T(8,128)S(1)} %bitcast.5, bf16[128,4096]{1,0:T(8,128)(2,1)S(1)} %copy-done.1), custom_call_target="tpu_custom_call" | custom-call | tf_op jit(solution)/shard_map/pallas_call | solution.py:366
  93.0 1.0 %copy.8 = bf16[128,4096]{1,0:T(8,128)(2,1)} copy(bf16[128,4096]{1,0:T(8,128)(2,1)S(1)} %shard_map.64) | data formatting | bytes 2097152
Async XLA Ops:
  0.0 1.4 %copy-start = (bf16[128,6144]{1,0:T(8,128)(2,1)S(1)}, bf16[128,6144]{1,0:T(8,128)(2,1)}, u32[]{:S(2)}) copy-start(bf16[128,6144]{1,0:T(8,128)(2,1)} %proj.1) | copy-start | bytes 4718596
  1.4 1.2 %copy-start.1 = (bf16[128,4096]{1,0:T(8,128)(2,1)S(1)}, bf16[128,4096]{1,0:T(8,128)(2,1)}, u32[]{:S(2)}) copy-start(bf16[128,4096]{1,0:T(8,128)(2,1)} %w_in.1) | copy-start | bytes 3145732
  2.6 0.9 copy-start.2
  3.5 0.9 copy-start.3
  4.4 0.9 copy-start.4
  5.3 0.7 copy-start.5

commit v2 on v1

--- a/solution.py
+++ b/solution.py
@@ -10,13 +10,17 @@
 MESH = pl.DeviceIdType.MESH
 LANES = 128
 PHASES = 4
-SKEW = 3
+LEVEL = 4
+PART = 4
+SKEW = 0
+PACE = (4, 1, 1, 1, 2, 2, 1, 1, 2, 2)
 
 
 def kernel(
-    ctx_count, proj, taps, pole, res, skip, w_in, out,
-    halo, pole_t, coef_t, decay, drive, filt, query, sent, came, gated, w_all, prod,
-    halo_sem, mate_sem, own_sem, ring_send, ring_recv, state_sem, gate_sem, fwd_sem, prod_sem, keep_sem,
+    ctx_count, proj_in, taps_in, pole_in, res_in, skip_in, w_in, out,
+    proj, taps, pole, res, skip,
+    halo, pole_t, coef_t, decay, drive, filt, query, sent, came, starts, origin, gated, w_all, prod,
+    load_sem, halo_sem, mate_sem, own_sem, ring_send, ring_recv, state_sem, start_sem, gate_sem, fwd_sem, prod_sem, keep_sem,
 ):
     group = lax.axis_index("groups")
     ctx = lax.axis_index("ctx")
@@ -37,9 +41,8 @@
     w_rows = w_in.shape[0]
     width = w_in.shape[1] // 4
     cols = width // PHASES
-    hops = [1]
-    while hops[-1] * 2 < ctx_count:
-        hops.append(hops[-1] * 2)
+    workers = min(ctx_count, poles * tiles // 8)
+    share = poles * tiles // workers
 
     def place_at(r):
         r = (r + 2 * places) % places
@@ -50,12 +53,17 @@
     behind = 2 * place_at(rank - sign) + core
 
     barrier = pltpu.get_barrier_semaphore()
-    greeted = [(group, other), (across, ctx), (across, other), (group, ahead), (group, behind)]
-    for hop in hops:
-        greeted.append((group, (ctx + hop) % ctx_count))
-        greeted.append((group, (ctx + ctx_count - hop) % ctx_count))
+    greeted = [(across, ctx), (across, other)]
+    for step in range(1, ctx_count):
+        greeted.append((group, (ctx + step) % ctx_count))
     for device in greeted:
         pl.semaphore_signal(barrier, inc=1, device_id=device, device_id_type=MESH)
+    loads = []
+    for k, (src, dst) in enumerate(
+        ((pole_in, pole), (res_in, res), (skip_in, skip), (taps_in, taps), (proj_in, proj))
+    ):
+        loads.append(pltpu.make_async_copy(src, dst, load_sem.at[k]))
+        loads[-1].start()
     pl.semaphore_wait(barrier, len(greeted))
 
     def remote(src, dst, send, recv, device):
@@ -73,7 +81,7 @@
 
     edge = min(16, tokens)
     halo_copy = remote(
-        proj.at[pl.ds(tokens - edge, edge)], halo, halo_sem.at[0], halo_sem.at[1],
+        proj_in.at[pl.ds(tokens - edge, edge)], halo, halo_sem.at[0], halo_sem.at[1],
         (group, (ctx + 1) % ctx_count),
     )
 
@@ -87,17 +95,6 @@
 
     def part(q, s):
         return pl.ds(pl.multiple_of(q * width + s * cols, cols), cols)
-
-    mate_copies = []
-    own_copies = []
-    for s in range(PHASES):
-        mate_copies.append(begin(remote(
-            w_in.at[:, part(their_quarter, s)], w_all.at[s, my_rows],
-            mate_sem.at[0, s], mate_sem.at[1, s], (group, other),
-        )))
-        own = pltpu.make_async_copy(w_in.at[:, part(quarter, s)], w_all.at[s, my_rows], own_sem.at[s])
-        own.start()
-        own_copies.append(own)
 
     def ring_copy(d, s, t):
         if d == 0:
@@ -112,19 +109,35 @@
         return remote(src, dst, ring_send.at[d, s, t], ring_recv.at[d, s, t], device)
 
     ring = {}
+    mate_copies = []
+    own_copies = []
+    for s in range(PHASES):
+        ring[0, s, 0] = begin(ring_copy(0, s, 0))
+        mate_copies.append(begin(remote(
+            w_in.at[:, part(their_quarter, s)], w_all.at[s, my_rows],
+            mate_sem.at[0, s], mate_sem.at[1, s], (group, other),
+        )))
+        own = pltpu.make_async_copy(w_in.at[:, part(quarter, s)], w_all.at[s, my_rows], own_sem.at[s])
+        own_copies.append(own)
+    for own in own_copies:
+        own.start()
+
 
     def event(s, t):
         for d in range(2):
+            if t == 0 and d == 0:
+                continue
             if t > 0:
                 ring[d, s, t - 1].wait_recv()
-            elif d == 1:
+            else:
                 mate_copies[s].wait_recv()
             if t < places - 1:
                 ring[d, s, t] = begin(ring_copy(d, s, t))
 
-    events = sorted(
-        [(t + SKEW * s, s, t) for s in range(PHASES) for t in range(places)]
-    )
+    def order(s, t):
+        return t + (SKEW * (s // 2) if t > LEVEL else 0)
+
+    events = sorted([(order(s, t), s, t) for s in range(PHASES) for t in range(places)])
     done = [0]
 
     def run_events(n):
@@ -135,9 +148,10 @@
                 done[0] += 1
 
     def phase_over(s):
-        return events.index((places - 1 + SKEW * s, s, places - 1)) + 1
-
-    run_events(3)
+        return events.index((order(s, places - 1), s, places - 1)) + 1
+
+    for load in loads:
+        load.wait()
 
     def spread(c, carry):
         lanes = pl.ds(pl.multiple_of(c * LANES, LANES), LANES)
@@ -160,6 +174,8 @@
 
     lax.fori_loop(0, tiles, spread, 0)
 
+    run_events(PACE[0])
+
     @pl.when(ctx > 0)
     def _():
         halo_copy.wait_recv()
@@ -200,65 +216,60 @@
         zero = tuple(jnp.zeros((8, LANES), jnp.float32) for _ in range(poles))
         state = lax.fori_loop(0, tokens, step, zero, unroll=4)
         for n in range(poles):
-            sent[0, n * tiles + h * 8 : n * tiles + h * 8 + 8] = state[n]
+            sent[n * tiles + h * 8 : n * tiles + h * 8 + 8] = state[n]
 
     for h in range(pieces):
         lax.fori_loop(h * 8, h * 8 + 8, make_drive, 0)
-        run_events(1)
+        run_events(PACE[2])
         end_state(h)
-        run_events(1)
-
-    def state_copy(slot, buf, hop):
-        return remote(
-            sent.at[buf], came.at[slot], state_sem.at[0, slot], state_sem.at[1, slot],
-            (group, (ctx + hop) % ctx_count),
-        )
-
-    state_copies = []
-
-    def state_start(slot, buf, hop):
-        copy = state_copy(slot, buf, hop)
-        state_copies.append((copy, hop))
-
-        @pl.when(ctx + hop < ctx_count)
-        def _():
-            copy.start()
-
-        return copy
-
-    first = state_start(0, 0, 1)
-    second = state_start(1, 0, 2)
-    run_events(1)
-    lax.fori_loop(0, tiles // 2, make_query, 0)
-    run_events(1)
-    sent[1] = jnp.zeros(sent.shape[1:], jnp.float32)
-
-    @pl.when(ctx >= 1)
-    def _():
-        first.wait_recv()
-        sent[1] = came[0]
-
-    @pl.when(ctx >= 2)
-    def _():
-        second.wait_recv()
-        sent[1] = sent[1] + decay[...] * came[1]
-
-    buf = 1
-    for k, hop in enumerate(hops[1:]):
-        copy = state_start(2 + k, buf, hop)
-        decay[...] = decay[...] * decay[...]
-        run_events(1)
-        if k == 0:
-            lax.fori_loop(tiles // 2, tiles, make_query, 0)
-        run_events(1)
-        sent[buf + 1] = sent[buf]
-
-        @pl.when(ctx >= hop)
-        def _():
-            copy.wait_recv()
-            sent[buf + 1] = sent[buf] + decay[...] * came[2 + k]
-
-        buf += 1
+        run_events(PACE[3])
+
+    def rows_of(index):
+        return pl.ds(pl.multiple_of(index * share, share), share)
+
+    def if_worker(index, body):
+        if workers == ctx_count:
+            body()
+        else:
+            pl.when(index < workers)(body)
+
+    at_step = [(ctx + step) % ctx_count for step in range(ctx_count)]
+    ends = [None]
+    begins = [None]
+    for step in range(1, ctx_count):
+        ends.append(remote(
+            sent.at[rows_of(at_step[step] % workers)], came.at[step],
+            state_sem.at[0, step], state_sem.at[1, step], (group, at_step[step]),
+        ))
+        begins.append(remote(
+            starts.at[at_step[step]], origin.at[rows_of(ctx % workers)],
+            start_sem.at[0, step], start_sem.at[1, step], (group, at_step[step]),
+        ))
+    for step in range(1, ctx_count):
+        if_worker(at_step[step], ends[step].start)
+    lax.fori_loop(0, tiles, make_query, 0)
+    run_events(PACE[4])
+
+    def combine():
+        mine = rows_of(ctx % workers)
+        came[0] = sent[mine]
+        for step in range(1, ctx_count):
+            ends[step].wait_recv()
+        fade = decay[mine]
+
+        def add(j, state):
+            starts[j] = state
+            return fade * state + came[(ctx + ctx_count - j) % ctx_count]
+
+        lax.fori_loop(0, ctx_count, add, jnp.zeros((share, LANES), jnp.float32))
+        origin[mine] = starts[ctx]
+        for step in range(1, ctx_count):
+            begins[step].start()
+
+    if_worker(ctx, combine)
+    run_events(PACE[5])
+    for step in range(1, ctx_count):
+        if_worker((ctx + ctx_count - step) % ctx_count, begins[step].wait_recv)
 
     def respond(h):
         p = [pole_t[n * tiles + h * 8 : n * tiles + h * 8 + 8] for n in range(poles)]
@@ -275,7 +286,7 @@
             filt[at] = terms[0]
             return state
 
-        start = tuple(sent[buf, n * tiles + h * 8 : n * tiles + h * 8 + 8] for n in range(poles))
+        start = tuple(origin[n * tiles + h * 8 : n * tiles + h * 8 + 8] for n in range(poles))
         lax.fori_loop(0, tokens, step, start, unroll=2)
 
     def gate(c, carry):
@@ -285,28 +296,30 @@
         return carry
 
     slot_across = (quarter + 2) % 4
-    span = chans // pieces
+    parts = tiles // PART
+    span = PART * LANES
     direct_copies = []
     for h in range(pieces):
         respond(h)
-        lax.fori_loop(h * 8, h * 8 + 8, gate, 0)
-        mine = gated.at[quarter, :, h * span : (h + 1) * span]
-        direct_copies.append((
-            begin(remote(mine, mine, gate_sem.at[0, 0, h], gate_sem.at[1, 0, h], (across, ctx))),
-            begin(remote(mine, mine, gate_sem.at[0, 1, h], gate_sem.at[1, 1, h], (group, other))),
-        ))
-        run_events(2)
+        for u in range(h * 8 // PART, (h + 1) * 8 // PART):
+            lax.fori_loop(u * PART, (u + 1) * PART, gate, 0)
+            mine = gated.at[quarter, :, u * span : (u + 1) * span]
+            direct_copies.append((
+                begin(remote(mine, mine, gate_sem.at[0, 0, u], gate_sem.at[1, 0, u], (across, ctx))),
+                begin(remote(mine, mine, gate_sem.at[0, 1, u], gate_sem.at[1, 1, u], (group, other))),
+            ))
+        run_events(PACE[6 + h % 2])
 
     forwards = []
-    for h in range(pieces):
-        run_events(3)
-        direct_copies[h][0].wait_recv()
-        theirs = gated.at[slot_across, :, h * span : (h + 1) * span]
-        forwards.append(begin(remote(theirs, theirs, fwd_sem.at[0, h], fwd_sem.at[1, h], (group, other))))
-    run_events(2)
-    for h in range(pieces):
-        direct_copies[h][1].wait_recv()
-        forwards[h].wait_recv()
+    for u in range(parts):
+        run_events(PACE[8])
+        direct_copies[u][0].wait_recv()
+        theirs = gated.at[slot_across, :, u * span : (u + 1) * span]
+        forwards.append(begin(remote(theirs, theirs, fwd_sem.at[0, u], fwd_sem.at[1, u], (group, other))))
+    run_events(PACE[9])
+    for u in range(parts):
+        direct_copies[u][1].wait_recv()
+        forwards[u].wait_recv()
 
     mates = [(group, other), (across, ctx), (across, other)]
     mate_slots = [(group % 2) * 2 + 1 - core, slot_across, (across % 2) * 2 + 1 - core]
@@ -343,11 +356,9 @@
     def _():
         halo_copy.wait_send()
 
-    for copy, hop in state_copies:
-
-        @pl.when(ctx + hop < ctx_count)
-        def _():
-            copy.wait_send()
+    for step in range(1, ctx_count):
+        if_worker(at_step[step], ends[step].wait_send)
+        if_worker(ctx, begins[step].wait_send)
 
 
 def local(ctx_count, projected, short_filter, modal_pole, residue, skip_weight, out_weight):
@@ -357,18 +368,22 @@
     tiles = chans // LANES
     cols = width // 4 // PHASES
     places = ctx_count // 2
-    hop_count = (ctx_count - 1).bit_length()
+    workers = min(ctx_count, poles * tiles // 8)
+    share = poles * tiles // workers
     dma = pltpu.SemaphoreType.DMA
-    whole = pl.BlockSpec(memory_space=pltpu.VMEM)
-    anywhere = pl.BlockSpec(memory_space=pl.ANY)
+    hbm = pl.BlockSpec(memory_space=pltpu.HBM)
     f32, bf16 = jnp.float32, jnp.bfloat16
-    pieces = tiles // 8
     return pl.pallas_call(
         functools.partial(kernel, ctx_count),
         out_shape=jax.ShapeDtypeStruct((tokens, width), bf16),
-        in_specs=[whole] * 5 + [anywhere],
-        out_specs=anywhere,
+        in_specs=[hbm] * 6,
+        out_specs=hbm,
         scratch_shapes=[
+            pltpu.VMEM((tokens, 3 * chans), bf16),
+            pltpu.VMEM(short_filter.shape, f32),
+            pltpu.VMEM((poles, chans), f32),
+            pltpu.VMEM((poles, chans), f32),
+            pltpu.VMEM((tiles, LANES), f32),
             pltpu.VMEM((min(16, tokens), 3 * chans), bf16),
             pltpu.VMEM((poles * tiles, LANES), f32),
             pltpu.VMEM((poles * tiles, LANES), f32),
@@ -376,24 +391,28 @@
             pltpu.VMEM((tokens * tiles, LANES), f32),
             pltpu.VMEM((tokens * tiles, LANES), f32),
             pltpu.VMEM((tokens, chans), f32),
-            pltpu.VMEM((hop_count + 1, poles * tiles, LANES), f32),
-            pltpu.VMEM((hop_count + 1, poles * tiles, LANES), f32),
+            pltpu.VMEM((poles * tiles, LANES), f32),
+            pltpu.VMEM((ctx_count, share, LANES), f32),
+            pltpu.VMEM((ctx_count, share, LANES), f32),
+            pltpu.VMEM((poles * tiles, LANES), f32),
             pltpu.VMEM((4, tokens, chans), bf16),
             pltpu.VMEM((PHASES, chans, cols), bf16),
             pltpu.VMEM((PHASES, 4, tokens, cols), bf16),
+            dma((5,)),
             dma((2,)),
             dma((2, PHASES)),
             dma((PHASES,)),
             dma((2, PHASES, places - 1)),
             dma((2, PHASES, places - 1)),
-            dma((2, hop_count + 1)),
-            dma((2, 2, pieces)),
-            dma((2, pieces)),
+            dma((2, ctx_count)),
+            dma((2, ctx_count)),
+            dma((2, 2, tiles // PART)),
+            dma((2, tiles // PART)),
             dma((2, 3, PHASES)),
             dma((PHASES,)),
         ],
         compiler_params=pltpu.CompilerParams(
-            collective_id=0, has_side_effects=True, vmem_limit_bytes=40 * 1024 * 1024
+            collective_id=0, has_side_effects=True, vmem_limit_bytes=63 * 1024 * 1024
         ),
     )(
         projected, short_filter, modal_pole.T, residue.T,

time: 94.3 us -> 70.2 us (0.74)
  Pallas kernels: 87 us -> 67.8 us
  local copies, waits for them, and re-layouts: 7 us -> 2.29 us
    pallas_call x1, Pallas kernels: 87 us -> 67.8 us  [local(): pl.pallas_call(functools.partial(kernel, ctx_count), out_shape=jax.ShapeD...]
    unnamed x13 -> x1, local copies, waits for them, and re-layouts: 7 us -> 2.29 us
where the time goes in v2:
time: 70.2 us; the launch traced here: 70.1 us
  Pallas kernels  67.8 us (97%)
  local copies, waits for them, and re-layouts  2.29 us (3%)
    pallas_call x1, Pallas kernels, local(): pl.pallas_call(functools.partial(kernel, ctx_count), out_shape=jax.ShapeD...  67.8 us
    unnamed x1, local copies, waits for them, and re-layouts  2.29 us

profile of v2, /device:TPU:1, one launch (start us, length us, event | category | flops | bytes accessed | tf_op | source)
XLA Modules:
  0.0 70.1 jit_solution(13452859434563965308)
XLA Ops:
  0.0 67.8 %shard_map.64 = bf16[128,4096]{1,0:T(8,128)(2,1)} custom-call(bf16[128,6144]{1,0:T(8,128)(2,1)} %proj_in.1, f32[3,6144]{1,0:T(4,128)} %taps_in.1, f32[16,2048]{1,0:T(8,128)} %bitcast.3, f32[16,2048]{1,0:T(8,128)} %bitcast.4, f32[16,128]{1,0:T(8,128)} %bitcast.5, bf16[128,4096]{1,0:T(8,128)(2,1)} %w_in.1), custom_call_target="tpu_custom_call" | custom-call | tf_op jit(solution)/shard_map/pallas_call | solution.py:376
  67.8 2.3 %copy.8 = bf16[128,4096]{1,0:T(8,128)(2,1)} copy(bf16[128,4096]{1,0:T(8,128)(2,1)} %shard_map.64) | data formatting | bytes 2097152

commit v3 on v2

--- a/solution.py
+++ b/solution.py
@@ -13,7 +13,7 @@
 LEVEL = 4
 PART = 4
 SKEW = 0
-PACE = (4, 1, 1, 1, 2, 2, 1, 1, 2, 2)
+PACE = (4, 1, 2, 1, 3, 3, 2, 2, 2, 2)
 
 
 def kernel(
@@ -112,13 +112,14 @@
     mate_copies = []
     own_copies = []
     for s in range(PHASES):
-        ring[0, s, 0] = begin(ring_copy(0, s, 0))
         mate_copies.append(begin(remote(
             w_in.at[:, part(their_quarter, s)], w_all.at[s, my_rows],
             mate_sem.at[0, s], mate_sem.at[1, s], (group, other),
         )))
         own = pltpu.make_async_copy(w_in.at[:, part(quarter, s)], w_all.at[s, my_rows], own_sem.at[s])
         own_copies.append(own)
+    for s in range(PHASES):
+        ring[0, s, 0] = begin(ring_copy(0, s, 0))
     for own in own_copies:
         own.start()
 

time: 70.2 us -> 68.7 us (0.979)
  Pallas kernels: 67.8 us -> 65.9 us
    pallas_call x1, Pallas kernels: 67.8 us -> 65.9 us  [local(): pl.pallas_call(functools.partial(kernel, ctx_count), out_shape=jax.ShapeD...]
where the time goes in v3:
time: 68.7 us; the launch traced here: 68.2 us
  Pallas kernels  65.9 us (96%)
  local copies, waits for them, and re-layouts  2.29 us (3%)
    pallas_call x1, Pallas kernels, local(): pl.pallas_call(functools.partial(kernel, ctx_count), out_shape=jax.ShapeD...  65.9 us
    unnamed x1, local copies, waits for them, and re-layouts  2.29 us

profile of v3, /device:TPU:1, one launch (start us, length us, event | category | flops | bytes accessed | tf_op | source)
XLA Modules:
  0.0 68.2 jit_solution(10485128768821021807)
XLA Ops:
  0.0 65.9 %shard_map.64 = bf16[128,4096]{1,0:T(8,128)(2,1)} custom-call(bf16[128,6144]{1,0:T(8,128)(2,1)} %proj_in.1, f32[3,6144]{1,0:T(4,128)} %taps_in.1, f32[16,2048]{1,0:T(8,128)} %bitcast.3, f32[16,2048]{1,0:T(8,128)} %bitcast.4, f32[16,128]{1,0:T(8,128)} %bitcast.5, bf16[128,4096]{1,0:T(8,128)(2,1)} %w_in.1), custom_call_target="tpu_custom_call" | custom-call | tf_op jit(solution)/shard_map/pallas_call | solution.py:377
  65.9 2.3 %copy.8 = bf16[128,4096]{1,0:T(8,128)(2,1)} copy(bf16[128,4096]{1,0:T(8,128)(2,1)} %shard_map.64) | data formatting | bytes 2097152
